TPU v7x, 32 devices: a whole 2x2x4 slice. The times are simulated.
32 devices in a mesh: fsdp: 4 (over y, x), tp: 4 (over z), tower: 2 (over core).
Axes of the slice: x: 2, y: 2, z: 4, core: 2. Of those that a mesh axis runs over, the one named last changes fastest.
Arguments:
- images: bfloat16 [4096, 5120], P(('fsdp', 'tower')), may hold values from -61 to 61
- img_weight: bfloat16 [5120, 1024], P('fsdp', 'tp')
- texts: bfloat16 [4096, 1024], P(('fsdp', 'tp', 'tower')), may hold values from -1 to 1
- pair_perm: int32 [4096], P(('fsdp', 'tower')), may hold values from 0 to 4095, as said below
- forget: int32 [4096], P(('fsdp', 'tower')), may hold values 0 or 1
Outputs:
- pair_loss: float32 [4096], P(('fsdp', 'tower'))
- weight_grad: float32 [5120, 1024], P('fsdp', 'tp')
Inputs may be any that keep to these rules, and one draw needn't show every extreme that they name: `pair_perm`: each number 0 to 4095 appears once.
All inputs are finite; a program needn't handle non-finite values. No bound on the sum of `forget` on one device may be relied on, other than what follows from the above.
Results may differ from a plain program's by a relative error of at most 0.0036.
Values may be sent and summed in bfloat16 or wider, within the bound.
A program may use at most 64 MiB of HBM per device.

v0:
```python
import jax
import jax.numpy as jnp
from jax import lax
from jax.sharding import PartitionSpec as P

epsilon = 1e-06
score_scale = 100.0


def combined_all(x, axis, combine):
    everything = jax.tree.map(lambda part: lax.all_gather(part, axis), x)
    first = jax.tree.map(lambda part: part[0], everything)

    def lap(k, so_far):
        return combine(so_far, jax.tree.map(lambda part: part[k], everything))

    return lax.fori_loop(1, lax.axis_size(axis), lap, first)


def local(images, img_weight, texts, pair_perm, forget):
    part = images
    emb_part = jnp.dot(
        part,
        lax.all_gather(img_weight, "fsdp", axis=0, tiled=True),
        preferred_element_type=jnp.float32,
    ).astype(jnp.bfloat16)
    emb = lax.all_gather(emb_part, "tp", axis=1, tiled=True)
    efloat = emb.astype(jnp.float32)
    rnorm = lax.rsqrt(jnp.sum(efloat * efloat, axis=1, keepdims=True) + epsilon)
    unit = efloat * rnorm
    unit_b = unit.astype(jnp.bfloat16)
    signs = 1.0 - 2.0 * forget.astype(jnp.float32)
    tp_index = lax.axis_index("tp")
    tp_count = lax.axis_size("tp")
    span = texts.shape[0] * lax.axis_size("tower")
    gathered = lax.all_gather(texts, ("fsdp", "tower"), axis=0, tiled=True)
    logits = score_scale * lax.dot_general(
        unit_b, gathered, (((1,), (1,)), ((), ())), preferred_element_type=jnp.float32
    )
    positions = 0 + jnp.arange(gathered.shape[0], dtype=jnp.int32)
    hit = (
        pair_perm[:, None]
        == ((positions // span * tp_count + tp_index) * span + positions % span)[None, :]
    )
    logits, hit = (logits, hit)
    top = jnp.max(logits, axis=1)
    total = jnp.sum(jnp.exp(logits - top[:, None]), axis=1)
    positive = jnp.sum(jnp.where(hit, logits, 0.0), axis=1)

    def combine(first, second):
        joined = jnp.maximum(first[0], second[0])
        summed = first[1] * jnp.exp(first[0] - joined) + second[1] * jnp.exp(second[0] - joined)
        return (joined, summed, first[2] + second[2])

    top, total, positive = combined_all((top, total, positive), "tp", combine)
    lse = top + jnp.log(total)
    pair_loss = lse - positive
    grad_part = score_scale * jnp.dot(
        (signs[:, None] * (jnp.exp(logits - lse[:, None]) - hit.astype(jnp.float32))).astype(
            jnp.bfloat16
        ),
        gathered,
        preferred_element_type=jnp.float32,
    )
    grad_unit = lax.psum_scatter(grad_part, "tp", scatter_dimension=1, tiled=True)
    unit_part = emb_part.astype(jnp.float32) * rnorm
    radial = lax.psum(jnp.sum(unit_part * grad_unit, axis=1, keepdims=True), "tp")
    grad_emb = (rnorm * (grad_unit - unit_part * radial)).astype(jnp.bfloat16)
    part = images
    share = lax.psum_scatter(
        lax.dot_general(
            part, grad_emb, (((0,), (0,)), ((), ())), preferred_element_type=jnp.float32
        ),
        "fsdp",
        scatter_dimension=0,
        tiled=True,
    )
    weight_grad = lax.psum(share, "tower")
    return (pair_loss, weight_grad)


def solution(mesh):
    return jax.shard_map(
        local,
        mesh=mesh,
        in_specs=(
            P(("fsdp", "tower"), None),
            P("fsdp", "tp"),
            P(("fsdp", "tp", "tower"), None),
            P(("fsdp", "tower")),
            P(("fsdp", "tower")),
        ),
        out_specs=(P(("fsdp", "tower")), P("fsdp", "tp")),
        check_vma=False,
    )
```

profile of v0, /device:TPU:9, one launch (start us, length us, event | category | flops | bytes accessed | tf_op | source)
XLA Modules:
  0.0 310.1 jit_solution(9285754020338744125)
XLA Ops:
  7.2 0.0 all-gather.10.cloned.1.call-start
  7.2 0.7 all-gather.10.cloned.1.call-update
  7.9 0.0 copy-start.1
  7.9 0.0 all-gather.12.cloned.1.call-start
  8.0 42.7 %all-gather.10.cloned.1.call-done = bf16[5120,256]{1,0:T(8,128)(2,1)} async-done(((bf16[1280,256]{1,0:T(8,128)(2,1)}), bf16[5120,256]{1,0:T(8,128)(2,1)}) %all-gather.10.cloned.1.call-update) | async-done | bytes 2621456 | tf_op jit(solution)/shard_map/all_gather | solution.py:24
  50.7 5.6 %convolution_convert_fusion = bf16[512,256]{0,1:T(8,128)(2,1)} fusion(bf16[512,5120]{1,0:T(8,128)(2,1)} %param.7, bf16[5120,256]{1,0:T(8,128)(2,1)} %all-gather.10.cloned.1.call-done), kind=kOutput, calls=%fused_computation.18 | convolution fusion | flops 1342308352 | bytes 8126464 | tf_op jit(solution)/shard_map/dot_general | solution.py:22
  56.3 0.0 all-gather.12.cloned.1.call-update
  56.3 0.0 all-gather.14.cloned.1.call-start
  56.3 0.7 all-gather.14.cloned.1.call-update
  57.0 0.0 reduce-scatter.3.cloned.1.call-start
  57.1 0.0 copy-done.1
  57.1 27.0 %all-gather.12.cloned.1.call-done = bf16[512,1024]{0,1:T(8,128)(2,1)} async-done(((bf16[512,256]{0,1:T(8,128)(2,1)}), bf16[512,1024]{0,1:T(8,128)(2,1)}) %all-gather.12.cloned.1.call-update) | async-done | bytes 1048592 | tf_op jit(solution)/shard_map/all_gather | solution.py:27
  84.1 1.5 fusion
  85.6 0.0 copy-start.2
  85.6 28.5 %all-gather.14.cloned.1.call-done = bf16[1024,1024]{1,0:T(8,128)(2,1)} async-done(((bf16[128,1024]{1,0:T(8,128)(2,1)}), bf16[1024,1024]{1,0:T(8,128)(2,1)}) %all-gather.14.cloned.1.call-update) | async-done | bytes 2097168 | tf_op jit(solution)/shard_map/all_gather | solution.py:36
  114.1 3.1 %multiply_reduce_fusion = (f32[512]{0:T(512)S(1)}, f32[512,1024]{0,1:T(8,128)S(1)}) fusion(bf16[1024,1024]{1,0:T(8,128)(2,1)} %all-gather.14.cloned.1.call-done, bf16[512,1024]{0,1:T(8,128)(2,1)} %all-gather.12.cloned.1.call-done, f32[512]{0:T(512)S(1)} %add_rsqrt_fusion), kind=kOutput, calls=%fused_computation.16 | convolution fusion | flops 1076362752 | bytes 5246976 | tf_op jit(solution)/shard_map/dot_general | solution.py:37
  117.2 9.3 %all-gather.3 = f32[4,1,512]{2,1,0:T(1,128)S(1)} all-gather(f32[1,1,512]{2,1,0:T(1,128)S(1)} %bitcast.40), channel_id=2, replica_groups=mesh['fsdp'=4,'tp'=4,'tower'=2] {'tp'}, dimensions={0}, use_global_device_ids=true | all-gather | bytes 10240 | tf_op jit(solution)/shard_map/all_gather | solution.py:11
  126.6 0.0 copy-done.2
  126.6 0.6 fusion.2
  127.2 8.3 %all-gather.4 = f32[4,1,512]{2,1,0:T(1,128)S(1)} all-gather(f32[1,1,512]{2,1,0:T(1,128)S(1)} %bitcast.42), channel_id=3, replica_groups=mesh['fsdp'=4,'tp'=4,'tower'=2] {'tp'}, dimensions={0}, use_global_device_ids=true | all-gather | bytes 10240 | tf_op jit(solution)/shard_map/all_gather | solution.py:11
  135.5 8.3 %all-gather.5 = f32[4,1,512]{2,1,0:T(1,128)S(1)} all-gather(f32[1,1,512]{2,1,0:T(1,128)S(1)} %bitcast.41), channel_id=4, replica_groups=mesh['fsdp'=4,'tp'=4,'tower'=2] {'tp'}, dimensions={0}, use_global_device_ids=true | all-gather | bytes 10240 | tf_op jit(solution)/shard_map/all_gather | solution.py:11
  143.8 0.3 while.19
  144.1 0.6 fusion.29
  144.7 4.5 %convolution_multiply_fusion = f32[512,1024]{0,1:T(8,128)} fusion(bf16[1024,1024]{1,0:T(8,128)(2,1)} %all-gather.14.cloned.1.call-done, f32[512,1024]{0,1:T(8,128)S(1)} %get-tuple-element.210, f32[512]{0:T(512)S(1)} %get-tuple-element.206, f32[512]{0:T(512)S(1)} %multiply_subtract_fusion, s32[512]{0:T(512)S(1)} %copy-done.2, s32[1024]{0:T(1024)S(1)} %fusion.26), kind=kOutput, calls=%fused_computation.17 | convolution fusion | flops 1077936128 | bytes 6301696 | tf_op jit(solution)/shard_map/dot_general | solution.py:58
  149.1 0.0 copy-start
  149.1 0.0 reduce-scatter.3.cloned.1.call-update
  149.2 0.0 reduce-scatter.5.cloned.1.call-start
  149.2 48.4 %reduce-scatter.3.cloned.1.call-done = f32[512,256]{0,1:T(8,128)} async-done(((f32[512,1024]{0,1:T(8,128)}), f32[512,256]{0,1:T(8,128)}) %reduce-scatter.3.cloned.1.call-update) | async-done | bytes 524304 | tf_op jit(solution)/shard_map/reduce_scatter | solution.py:65
  197.6 0.0 copy-done
  197.6 1.1 multiply_reduce_fusion.1
  198.8 9.1 %psum.14 = f32[512]{0:T(512)S(1)} all-reduce(f32[512]{0:T(512)S(1)} %multiply_reduce_fusion.1), channel_id=1, replica_groups=mesh['fsdp'=4,'tp'=4,'tower'=2] {'tp'}, use_global_device_ids=true, to_apply=%region_8.9 | all-reduce | flops 512 | bytes 4096 | tf_op jit(solution)/shard_map/psum | solution.py:67
  207.8 6.5 %convolution_bitcast_fusion = f32[5120,256]{0,1:T(8,128)} fusion(bf16[512,5120]{1,0:T(8,128)(2,1)} %param.7, f32[512,256]{0,1:T(8,128)} %reduce-scatter.3.cloned.1.call-done, bf16[512,256]{0,1:T(8,128)(2,1)S(1)} %copy-done, f32[512]{0:T(512)S(1)} %psum.14, f32[512]{0:T(512)S(1)} %add_rsqrt_fusion), kind=kOutput, calls=%fused_computation.4 | convolution fusion | flops 1342963712 | bytes 11276288 | tf_op jit(solution)/shard_map/dot_general | solution.py:71
  214.4 0.0 reduce-scatter.5.cloned.1.call-update
  214.4 0.0 all-reduce.2.cloned.1.call-start
  214.4 63.0 %reduce-scatter.5.cloned.1.call-done = f32[1280,256]{0,1:T(8,128)} async-done(((f32[5120,256]{0,1:T(8,128)}), f32[1280,256]{0,1:T(8,128)}) %reduce-scatter.5.cloned.1.call-update) | async-done | bytes 1310736 | tf_op jit(solution)/shard_map/reduce_scatter | solution.py:70
  277.5 0.0 all-reduce.2.cloned.1.call-update
  277.5 23.0 %all-reduce.2.cloned.1.call-done = f32[1280,256]{0,1:T(8,128)} async-done(((f32[1280,256]{0,1:T(8,128)}), f32[1280,256]{0,1:T(8,128)}) %all-reduce.2.cloned.1.call-update) | async-done | bytes 1310736 | tf_op jit(solution)/shard_map/psum | solution.py:78
  300.5 2.8 copy.12
  (21 shorter events, 0.2 us)
Async XLA Ops:
  7.2 43.5 %all-gather.10.cloned.1.call-start = ((), (), s32[]{:S(2)}) async-start(), calls=%async_computation.2 | async-start | bytes 3276800 | tf_op jit(solution)/shard_map/all_gather | solution.py:24
  7.9 49.2 %copy-start.1 = (s32[512]{0:T(512)S(1)}, s32[512]{0:T(512)}, u32[]{:S(2)}) copy-start(s32[512]{0:T(512)} %param.11) | copy-start | bytes 6148
  7.9 76.2 %all-gather.12.cloned.1.call-start = ((), (), s32[]{:S(2)}) async-start(), calls=%async_computation.3 | async-start | bytes 1310720 | tf_op jit(solution)/shard_map/all_gather | solution.py:27
  56.3 57.8 %all-gather.14.cloned.1.call-start = ((), (), s32[]{:S(2)}) async-start(), calls=%async_computation.4 | async-start | bytes 2359296 | tf_op jit(solution)/shard_map/all_gather | solution.py:36
  57.0 140.6 %reduce-scatter.3.cloned.1.call-start = ((), (), s32[]{:S(2)}) async-start(), calls=%async_computation.5 | async-start | bytes 2621440 | tf_op jit(solution)/shard_map/reduce_scatter | solution.py:65
  85.6 41.0 %copy-start.2 = (s32[512]{0:T(512)S(1)}, s32[512]{0:T(512)}, u32[]{:S(2)}) copy-start(s32[512]{0:T(512)} %param.10) | copy-start | bytes 6148
  149.1 48.5 %copy-start = (bf16[512,256]{0,1:T(8,128)(2,1)S(1)}, bf16[512,256]{0,1:T(8,128)(2,1)}, u32[]{:S(2)}) copy-start(bf16[512,256]{0,1:T(8,128)(2,1)} %convolution_convert_fusion) | copy-start | bytes 786436
  149.2 128.3 %reduce-scatter.5.cloned.1.call-start = ((), (), s32[]{:S(2)}) async-start(), calls=%async_computation.6 | async-start | bytes 6553600 | tf_op jit(solution)/shard_map/reduce_scatter | solution.py:70
  214.4 86.1 %all-reduce.2.cloned.1.call-start = ((), (), s32[]{:S(2)}) async-start(), calls=%async_computation.7 | async-start | bytes 2621440 | tf_op jit(solution)/shard_map/psum | solution.py:78
Sparse Core Ops, SparseCore 0:
  9.8 40.7 all-gather.9
  56.4 27.6 all-gather.11
  86.0 28.0 all-gather.13
  149.3 48.3 reduce-scatter.2
  214.5 62.9 reduce-scatter.4
  279.8 20.6 all-reduce.1
where the time goes:
time: 311 us; the launch traced here: 310 us
  waiting for transfers between devices  234 us (75%)
  blocking collectives  35 us (11%)
  matrix products  19.7 us (6%)
  between operations  14.2 us (5%)
  other arithmetic  3.92 us (1%)
    reduce_scatter x1, waiting for transfers between devices, local(): lax.psum_scatter(lax.dot_general(part, grad_emb, (((0,), (0,)), ((), ()))...  63 us
    reduce_scatter x1, waiting for transfers between devices, local(): lax.psum_scatter(grad_part, 'tp', scatter_dimension=1, tiled=True)  48.4 us
    all_gather x1, waiting for transfers between devices, local(): lax.all_gather(img_weight, 'fsdp', axis=0, tiled=True)  42.7 us
    all_gather x1, waiting for transfers between devices, local(): gathered = lax.all_gather(texts, ('fsdp', 'tower'), axis=0, tiled=True)  28.5 us
    all_gather x1, waiting for transfers between devices, local(): emb = lax.all_gather(emb_part, 'tp', axis=1, tiled=True)  27 us
    all_gather x3, blocking collectives, combined_all(): everything = jax.tree.map(lambda part: lax.all_gather(part, axis), x)  25.9 us
    psum x1, waiting for transfers between devices, local(): weight_grad = lax.psum(share, 'tower')  23 us
    psum x1, blocking collectives, local(): lax.psum(jnp.sum(unit_part * grad_unit, axis=1, keepdims=True), 'tp')  9.06 us
  transfers between devices with their start and end apart: 6, of which 6 were waited for; matrix products, arithmetic and copies ran while one was open for 0% of the time, Pallas kernels for 0%

commit v1 on v0

v1 whole, which is shorter than its diff:
```python
import functools

import jax
import jax.numpy as jnp
from jax import lax
from jax.experimental import pallas as pl
from jax.experimental.pallas import tpu as pltpu
from jax.sharding import PartitionSpec as P

epsilon = 1e-06
score_scale = 100.0
F32 = jnp.float32
BF16 = jnp.bfloat16
NT = (((1,), (1,)), ((), ()))


def spread(columns, lanes):
    n = columns[0].shape[1]
    which = lax.broadcasted_iota(jnp.int32, (lanes, n), 0)
    block = jnp.broadcast_to(columns[0], (lanes, n))
    for k in range(1, len(columns)):
        block = jnp.where(which == k, columns[k], block)
    block = block.T
    return [block[:, k : k + 1] for k in range(len(columns))]


def kernel(sizes, images, weight, texts, perm, forget, loss, out, *scratch):
    F, T, C, R = sizes
    (img, img_t, wall, tall, acc, ebuf, ubuf, lbuf, pbuf, sbuf, gown, gsend, grecv, gemb,
     share, sib_send, sib_recv, wsend, wrecv, obuf,
     loc, w_s, w_r, wf_s, wf_r, t_s, t_r, tf_s, tf_r, to_s, to_r, e_s, e_r, st_s, st_r,
     g_s, g_r, b_s, b_r, x_s, x_r, o_s, o_r) = scratch
    f, t, c = lax.axis_index("fsdp"), lax.axis_index("tp"), lax.axis_index("tower")
    pairs, width = img.shape
    kb, cols = weight.shape
    kh = kb // C
    tr, embed = texts.shape
    bw = tr * C
    rows = pairs // R
    sends = []

    def other(me, d, n):
        return lax.rem(me + d, n)

    def remote(src, dst, ssem, rsem, axis, target):
        return pltpu.make_async_remote_copy(
            src_ref=src, dst_ref=dst, send_sem=ssem, recv_sem=rsem,
            device_id={axis: target}, device_id_type=pl.DeviceIdType.MESH,
        )

    def send(*args):
        copy = remote(*args)
        copy.start()
        sends.append(copy)

    def arrived(dst, ssem, rsem, axis, target):
        remote(dst, dst, ssem, rsem, axis, target).wait_recv()

    def wpart(ff, cc):
        return wall.at[pl.ds(pl.multiple_of(ff * kb + cc * kh, 16), kh)]

    def tpart(ff, cc):
        return tall.at[ff, pl.ds(pl.multiple_of(cc * tr, 16), tr)]

    img_copy = pltpu.make_async_copy(images, img, loc.at[0])
    img_copy.start()
    w_copy = pltpu.make_async_copy(
        weight, wall.at[pl.ds(pl.multiple_of(f * kb, 16), kb)], loc.at[1])
    w_copy.start()
    t_copy = pltpu.make_async_copy(texts, tpart(f, c), loc.at[2])
    t_copy.start()

    barrier = pltpu.get_barrier_semaphore()
    for axis, me, n in (("fsdp", f, F), ("tp", t, T), ("tower", c, C)):
        for d in range(1, n):
            pl.semaphore_signal(barrier, inc=1, device_id={axis: other(me, d, n)},
                                device_id_type=pl.DeviceIdType.MESH)
    pl.semaphore_wait(barrier, F + T + C - 3)

    mine = weight.at[pl.ds(pl.multiple_of(c * kh, 16), kh)]
    for d in range(1, F):
        send(mine, wpart(f, c), w_s.at[d], w_r.at[d], "fsdp", other(f, d, F))
    for d in range(1, F):
        send(texts, tpart(f, c), t_s.at[d], t_r.at[d], "fsdp", other(f, d, F))
    for e in range(1, C):
        send(texts, tpart(f, c), to_s.at[e], to_r.at[e], "tower", other(c, e, C))

    img_copy.wait()
    w_copy.wait()
    aligned = kb % 128 == 0

    def by_k(ff):
        k = pl.multiple_of(ff * kb, kb)
        return jnp.dot(img[:, pl.ds(k, kb)], wall[pl.ds(k, kb), :], preferred_element_type=F32)

    if aligned:
        acc[...] = by_k(f)

    def turn(k, carry):
        k = pl.multiple_of(k * 128, 128)
        img_t[pl.ds(k, 128), :] = img[:, pl.ds(k, 128)].T
        return carry

    lax.fori_loop(0, width // 128, turn, 0)

    def w_from(d):
        ff = other(f, F - d, F)
        arrived(wpart(ff, c), w_s.at[d], w_r.at[d], "fsdp", ff)
        for e in range(1, C):
            send(wpart(ff, c), wpart(ff, c), wf_s.at[d, e], wf_r.at[d, e], "tower", other(c, e, C))

    def w_rest(d):
        ff = other(f, F - d, F)
        for e in range(1, C):
            cc = other(c, C - e, C)
            arrived(wpart(ff, cc), wf_s.at[d, e], wf_r.at[d, e], "tower", cc)
        if aligned:
            acc[...] += by_k(ff)

    for d in range(1, F):
        w_from(d)
        if d > 1:
            w_rest(d - 1)
    w_rest(F - 1)
    if not aligned:
        acc[...] = jnp.zeros_like(acc)

        def by_tile(k, carry):
            k = pl.multiple_of(k * 128, 128)
            acc[...] += jnp.dot(img[:, pl.ds(k, 128)], wall[pl.ds(k, 128), :],
                                preferred_element_type=F32)
            return carry

        lax.fori_loop(0, width // 128, by_tile, 0)

    for r in range(R):
        ebuf[r, t] = acc[r * rows : (r + 1) * rows, :].astype(BF16)
        for d in range(1, T):
            send(ebuf.at[r, t], ebuf.at[r, t], e_s.at[r, d], e_r.at[r, d], "tp", other(t, d, T))

    t_copy.wait()
    for d in range(1, F):
        ff = other(f, F - d, F)
        arrived(tpart(ff, c), t_s.at[d], t_r.at[d], "fsdp", ff)
        for e in range(1, C):
            send(tpart(ff, c), tpart(ff, c), tf_s.at[d, e], tf_r.at[d, e], "tower", other(c, e, C))
    for e in range(1, C):
        cc = other(c, C - e, C)
        arrived(tpart(f, cc), to_s.at[e], to_r.at[e], "tower", cc)
    for d in range(1, F):
        ff = other(f, F - d, F)
        for e in range(1, C):
            cc = other(c, C - e, C)
            arrived(tpart(ff, cc), tf_s.at[d, e], tf_r.at[d, e], "tower", cc)

    kept = []
    for r in range(R):
        for d in range(1, T):
            tt = other(t, T - d, T)
            arrived(ebuf.at[r, tt], e_s.at[r, d], e_r.at[r, d], "tp", tt)
        square = jnp.zeros((rows, 1), F32)
        for k in range(T):
            part = ebuf[r, k].astype(F32)
            square += jnp.sum(part * part, axis=1, keepdims=True)
        rnorm = lax.rsqrt(square + epsilon)
        for k in range(T):
            ubuf[:, k * cols : (k + 1) * cols] = (ebuf[r, k].astype(F32) * rnorm).astype(BF16)

        span = slice(r * rows, (r + 1) * rows)
        sign_row = 1.0 - 2.0 * forget[:, span].astype(F32)
        permf, = spread([perm[:, span].astype(F32)], 128)
        lane = lax.broadcasted_iota(jnp.int32, (1, bw), 1)

        def hits(j):
            return permf == ((j * T + t) * bw + lane).astype(F32)

        def score(j, top):
            logit = score_scale * lax.dot_general(ubuf[...], tall[j], NT, preferred_element_type=F32)
            lbuf[j] = logit
            return jnp.maximum(top, jnp.max(logit, axis=1, keepdims=True))

        top = lax.fori_loop(0, F, score, jnp.full((rows, 1), -jnp.inf, F32))

        def totals(j, so_far):
            total, first, positive = so_far
            logit = lbuf[j]
            power = jnp.exp(logit - top)
            return (
                total + jnp.sum(power, axis=1, keepdims=True),
                first + jnp.sum(power * logit, axis=1, keepdims=True),
                positive + jnp.sum(jnp.where(hits(j), logit, 0.0), axis=1, keepdims=True),
            )

        zero = jnp.zeros((rows, 1), F32)
        total, first, positive = lax.fori_loop(0, F, totals, (zero, zero, zero))
        place = lax.broadcasted_iota(jnp.int32, (rows, 128), 1)
        packed = jnp.where(place == 0, top, jnp.where(place == 1, total,
                           jnp.where(place == 2, first, positive)))
        sbuf[r, t] = packed.T[:8]
        for d in range(1, T):
            send(sbuf.at[r, t], sbuf.at[r, t], st_s.at[r, d], st_r.at[r, d], "tp", other(t, d, T))
        for d in range(1, T):
            tt = other(t, T - d, T)
            arrived(sbuf.at[r, tt], st_s.at[r, d], st_r.at[r, d], "tp", tt)
        peak = sbuf[r, 0, 0:1, :]
        for k in range(1, T):
            peak = jnp.maximum(peak, sbuf[r, k, 0:1, :])
        total = jnp.zeros_like(peak)
        first = jnp.zeros_like(peak)
        positive = jnp.zeros_like(peak)
        for k in range(T):
            scale = jnp.exp(sbuf[r, k, 0:1, :] - peak)
            total += scale * sbuf[r, k, 1:2, :]
            first += scale * sbuf[r, k, 2:3, :]
            positive += sbuf[r, k, 3:4, :]
        lse_row = peak + jnp.log(total)
        loss[:, span] = lse_row - positive
        lse, sign, radial = spread([lse_row, sign_row, sign_row * (first / total - positive)], 128)

        def weigh(j, carry):
            pbuf[j] = (sign * (jnp.exp(lbuf[j] - lse) - hits(j).astype(F32))).astype(BF16)
            return carry

        lax.fori_loop(0, F, weigh, 0)

        def grad_for(tt):
            place = pl.ds(pl.multiple_of(tt * cols, cols), cols)
            total = jnp.dot(pbuf[0], tall[0, :, place], preferred_element_type=F32)
            for j in range(1, F):
                total += jnp.dot(pbuf[j], tall[j, :, place], preferred_element_type=F32)
            return score_scale * total

        for d in range(1, T):
            tt = other(t, d, T)
            gsend[r, d] = grad_for(tt).astype(BF16)
            send(gsend.at[r, d], grecv.at[r, d], g_s.at[r, d], g_r.at[r, d], "tp", tt)
        gown[r] = grad_for(t)
        kept.append((rnorm, radial))

    for r in range(R):
        rnorm, radial = kept[r]
        grad = gown[r]
        for d in range(1, T):
            arrived(grecv.at[r, d], g_s.at[r, d], g_r.at[r, d], "tp", other(t, T - d, T))
            grad += grecv[r, d].astype(F32)
        unit = ebuf[r, t].astype(F32) * rnorm
        gemb[r * rows : (r + 1) * rows, :] = (rnorm * (grad - unit * radial)).astype(BF16)

    def block(ff, cc):
        k = pl.multiple_of(ff * kb + cc * kh, 16)
        return jnp.dot(img_t[pl.ds(k, kh), :], gemb[...], preferred_element_type=F32)

    def compute(d):
        ff = other(f, d, F)
        for e in range(1, C):
            cc = other(c, e, C)
            sib_send[d, e] = block(ff, cc)
            send(sib_send.at[d, e], sib_recv.at[d, e], b_s.at[d, e], b_r.at[d, e], "tower", cc)
        share[d] = block(ff, c)

    def joined(d):
        total = share[d]
        for e in range(1, C):
            arrived(sib_recv.at[d, e], b_s.at[d, e], b_r.at[d, e], "tower", other(c, C - e, C))
            total += sib_recv[d, e]
        return total

    def dispatch(d):
        wsend[d] = joined(d).astype(BF16)
        send(wsend.at[d], wrecv.at[d], x_s.at[d], x_r.at[d], "fsdp", other(f, d, F))

    for d in range(1, F):
        compute(d)
        if d > 1:
            dispatch(d - 1)
    compute(0)
    dispatch(F - 1)
    total = joined(0)
    for d in range(1, F):
        arrived(wrecv.at[d], x_s.at[d], x_r.at[d], "fsdp", other(f, F - d, F))
        total += wrecv[d].astype(F32)
    obuf[c] = total
    for e in range(1, C):
        send(obuf.at[c], obuf.at[c], o_s.at[e], o_r.at[e], "tower", other(c, e, C))
    home = pltpu.make_async_copy(obuf.at[c], out.at[c], loc.at[3])
    home.start()
    for e in range(1, C):
        cc = other(c, C - e, C)
        arrived(obuf.at[cc], o_s.at[e], o_r.at[e], "tower", cc)
        away = pltpu.make_async_copy(obuf.at[cc], out.at[cc], loc.at[3 + e])
        away.start()
        away.wait()
    home.wait()
    for copy in sends:
        copy.wait_send()


def local(images, weight, texts, perm, forget):
    F, T, C = lax.axis_size("fsdp"), lax.axis_size("tp"), lax.axis_size("tower")
    R = 2
    pairs, width = images.shape
    kb, cols = weight.shape
    kh = kb // C
    tr, embed = texts.shape
    rows = pairs // R
    bw = tr * C
    vmem, dma = pltpu.VMEM, pltpu.SemaphoreType.DMA
    scratch = [
        vmem((pairs, width), BF16),
        vmem((width, pairs), BF16),
        vmem((width, cols), BF16),
        vmem((F, bw, embed), BF16),
        vmem((pairs, cols), F32),
        vmem((R, T, rows, cols), BF16),
        vmem((rows, embed), BF16),
        vmem((F, rows, bw), F32),
        vmem((F, rows, bw), BF16),
        vmem((R, T, 8, rows), F32),
        vmem((R, rows, cols), F32),
        vmem((R, T, rows, cols), BF16),
        vmem((R, T, rows, cols), BF16),
        vmem((pairs, cols), BF16),
        vmem((F, kh, cols), F32),
        vmem((F, C, kh, cols), F32),
        vmem((F, C, kh, cols), F32),
        vmem((F, kh, cols), BF16),
        vmem((F, kh, cols), BF16),
        vmem((C, kh, cols), F32),
        dma((3 + C,)),
        dma((F,)), dma((F,)), dma((F, C)), dma((F, C)),
        dma((F,)), dma((F,)), dma((F, C)), dma((F, C)),
        dma((C,)), dma((C,)),
        dma((R, T)), dma((R, T)), dma((R, T)), dma((R, T)),
        dma((R, T)), dma((R, T)),
        dma((F, C)), dma((F, C)), dma((F,)), dma((F,)),
        dma((C,)), dma((C,)),
    ]
    any_space = pl.BlockSpec(memory_space=pl.ANY)
    whole = pl.BlockSpec(memory_space=pltpu.VMEM)
    loss, out = pl.pallas_call(
        functools.partial(kernel, (F, T, C, R)),
        out_shape=(
            jax.ShapeDtypeStruct((1, pairs), F32),
            jax.ShapeDtypeStruct((C, kh, cols), F32),
        ),
        in_specs=[any_space, any_space, any_space, whole, whole],
        out_specs=(whole, any_space),
        scratch_shapes=scratch,
        compiler_params=pltpu.CompilerParams(
            collective_id=0, has_side_effects=True, vmem_limit_bytes=56 * 2**20
        ),
        cost_estimate=pl.CostEstimate(
            flops=4 * pairs * cols * width + 4 * pairs * F * bw * embed,
            bytes_accessed=2 * (pairs * width + kb * cols + tr * embed) + 4 * kb * cols,
            transcendentals=2 * pairs * F * bw,
        ),
    )(images, weight, texts, perm.reshape(1, pairs), forget.reshape(1, pairs))
    return loss.reshape(pairs), out.reshape(kb, cols)


def solution(mesh):
    return jax.shard_map(
        local,
        mesh=mesh,
        in_specs=(
            P(("fsdp", "tower"), None),
            P("fsdp", "tp"),
            P(("fsdp", "tp", "tower"), None),
            P(("fsdp", "tower")),
            P(("fsdp", "tower")),
        ),
        out_specs=(P(("fsdp", "tower")), P("fsdp", "tp")),
        check_vma=False,
    )
```

time: 311 us -> 106 us (0.34)
  waiting for transfers between devices: 234 us -> 0 us
  Pallas kernels: 0 us -> 101 us
  blocking collectives: 35 us -> 0 us
  matrix products: 19.7 us -> 0 us
  between operations: 14.2 us -> 0.64 us
  other arithmetic: 3.92 us -> 0 us
    reduce_scatter x2 -> x0, waiting for transfers between devices: 111 us -> none  [the longest x1 63 us: local(): lax.psum_scatter(lax.dot_general(part, grad_emb, (((0,), (0,)), ((), ()))...]
    pallas_call x0 -> x1, Pallas kernels: none -> 101 us  [local(): pl.pallas_call(functools.partial(kernel, (F, T, C, R)), out_shape=(jax.Sh...]
    all_gather x3 -> x0, waiting for transfers between devices: 98.2 us -> none  [the longest x1 42.7 us: local(): lax.all_gather(img_weight, 'fsdp', axis=0, tiled=True)]
    all_gather x3 -> x0, blocking collectives: 25.9 us -> none  [combined_all(): everything = jax.tree.map(lambda part: lax.all_gather(part, axis), x)]
    psum x1 -> x0, waiting for transfers between devices: 23 us -> none  [local(): weight_grad = lax.psum(share, 'tower')]
    dot_general x4 -> x0, matrix products: 19.7 us -> none  [the longest x1 6.51 us: local(): lax.dot_general(part, grad_emb, (((0,), (0,)), ((), ())), preferred_eleme...]
    psum x1 -> x0, blocking collectives: 9.06 us -> none  [local(): lax.psum(jnp.sum(unit_part * grad_unit, axis=1, keepdims=True), 'tp')]
    reduce_sum x3 -> x0, other arithmetic: 3.22 us -> none  [the longest x1 1.5 us: local(): rnorm = lax.rsqrt(jnp.sum(efloat * efloat, axis=1, keepdims=True) + epsilon)]
  transfers between devices with their start and end apart: 6 -> 0, of which waited for: 6 -> 0; matrix products, arithmetic and copies ran while one was open for 0% -> 0% of each run, Pallas kernels for 0% -> 0%
where the time goes in v1:
time: 106 us; the launch traced here: 105 us
  Pallas kernels  101 us (95%)
  local copies, waits for them, and re-layouts  3.71 us (4%)
    pallas_call x1, Pallas kernels, local(): pl.pallas_call(functools.partial(kernel, (F, T, C, R)), out_shape=(jax.Sh...  101 us
    unnamed x2, local copies, waits for them, and re-layouts  3.71 us

profile of v1, /device:TPU:9, one launch (start us, length us, event | category | flops | bytes accessed | tf_op | source)
XLA Modules:
  0.0 105.1 jit_solution(12775250652128757483)
XLA Ops:
  0.6 100.8 %shard_map.68 = (f32[1,512]{1,0:T(1,128)}, f32[2,640,256]{2,1,0:T(8,128)}) custom-call(bf16[512,5120]{1,0:T(8,128)(2,1)} %images.1, bf16[1280,256]{1,0:T(8,128)(2,1)} %weight.1, bf16[128,1024]{1,0:T(8,128)(2,1)} %texts.1, s32[1,512]{1,0:T(1,128)} %bitcast.6, s32[1,512]{1,0:T(1,128)} %bitcast.7), custom_call_target="tpu_custom_call" | custom-call | flops 4831838208 | bytes 7471104 | tf_op jit(solution)/shard_map/pallas_call | solution.py:340
  101.4 1.3 %copy.9 = f32[512]{0:T(512)} copy(f32[512]{0:T(512)} %bitcast.5) | data formatting | bytes 4096
  102.7 2.5 %copy.10 = f32[1280,256]{1,0:T(8,128)} copy(f32[1280,256]{1,0:T(8,128)} %bitcast.4) | data formatting | bytes 2621440

commit v2 on v1

v2 whole, which is shorter than its diff:
```python
import functools

import jax
import jax.numpy as jnp
from jax import lax
from jax.experimental import pallas as pl
from jax.experimental.pallas import tpu as pltpu
from jax.sharding import PartitionSpec as P

epsilon = 1e-06
score_scale = 100.0
F32 = jnp.float32
BF16 = jnp.bfloat16
NT = (((1,), (1,)), ((), ()))


def spread(columns, lanes):
    n = columns[0].shape[1]
    which = lax.broadcasted_iota(jnp.int32, (lanes, n), 0)
    block = jnp.broadcast_to(columns[0], (lanes, n))
    for k in range(1, len(columns)):
        block = jnp.where(which == k, columns[k], block)
    block = block.T
    return [block[:, k : k + 1] for k in range(len(columns))]


def kernel(sizes, images, weight, texts, perm, forget, loss, out, *scratch):
    F, T, C = sizes
    (img, img_t, wall, tall, acc, eown, ebuf, ubuf, lbuf, pbuf, sbuf, gown, gsend, grecv, gemb,
     share, sib_send, sib_recv, wsend, wrecv, obuf,
     loc, w_s, w_r, wf_s, wf_r, t_s, t_r, tf_s, tf_r, to_s, to_r, tp_s, tp_r, e_s, e_r, st_s, st_r,
     g_s, g_r, b_s, b_r, x_s, x_r, o_s, o_r) = scratch
    f, t, c = lax.axis_index("fsdp"), lax.axis_index("tp"), lax.axis_index("tower")
    q, h = lax.div(t, 2), lax.rem(t, 2)
    pairs, width = img.shape
    half = pairs // 2
    kb, cols = weight.shape
    kh = kb // C
    tr, embed = texts.shape
    bw = 2 * tr * C
    square_plane = F == 4
    sends = []

    def other(me, d, n):
        return lax.rem(me + d, n)

    def fsdp_to(d):
        if not square_plane:
            return lax.rem(f + d, F)
        high, low = lax.div(f, 2), lax.rem(f, 2)
        return 2 * (1 - high if d & 2 else high) + (1 - low if d & 1 else low)

    def fsdp_from(d):
        return fsdp_to(d) if square_plane else lax.rem(f + F - d, F)

    def remote(src, dst, ssem, rsem, axis, target):
        return pltpu.make_async_remote_copy(
            src_ref=src, dst_ref=dst, send_sem=ssem, recv_sem=rsem,
            device_id={axis: target}, device_id_type=pl.DeviceIdType.MESH,
        )

    def send(*args):
        copy = remote(*args)
        copy.start()
        sends.append(copy)

    def arrived(dst, ssem, rsem, axis, target):
        remote(dst, dst, ssem, rsem, axis, target).wait_recv()

    def gather_start(mine, part, size, ssem, rsem):
        for d in (1, 2) if square_plane else range(1, F):
            send(mine, part(f, 0, size), ssem(d), rsem(d), "fsdp", fsdp_to(d))

    def gather_wait(d, part, size, ssem, rsem):
        ff = fsdp_from(d)
        if not square_plane:
            arrived(part(ff, 0, size), ssem(d), rsem(d), "fsdp", ff)
        elif d < 3:
            arrived(part(ff, 0, size), ssem(d), rsem(d), "fsdp", ff)
            piece = part(ff, (d - 1) * (size // 2), size // 2)
            send(piece, piece, ssem(2 + d), rsem(2 + d), "fsdp", fsdp_to(3 - d))
        else:
            for k in (0, 1):
                arrived(part(ff, k * (size // 2), size // 2), ssem(3 + k), rsem(3 + k),
                        "fsdp", fsdp_from(2 - k))

    def share_out(block, ssem, rsem):
        for e in range(1, C):
            send(block, block, ssem(e), rsem(e), "tower", other(c, e, C))

    def shared_in(block, ssem, rsem):
        for e in range(1, C):
            cc = other(c, C - e, C)
            arrived(block(cc), ssem(e), rsem(e), "tower", cc)

    def wpart(cc):
        return lambda ff, lo, n: wall.at[pl.ds(pl.multiple_of(ff * kb + cc * kh + lo, 16), n)]

    def tpart(p, cc):
        return lambda ff, lo, n: tall.at[ff, pl.ds(pl.multiple_of((p * C + cc) * tr + lo, 16), n)]

    img_copy = pltpu.make_async_copy(images, img, loc.at[0])
    img_copy.start()
    w_copy = pltpu.make_async_copy(
        weight, wall.at[pl.ds(pl.multiple_of(f * kb, 16), kb)], loc.at[1])
    w_copy.start()
    t_copy = pltpu.make_async_copy(texts, tpart(h, c)(f, 0, tr), loc.at[2])
    t_copy.start()

    barrier = pltpu.get_barrier_semaphore()
    for axis, me, n in (("fsdp", f, F), ("tp", t, T), ("tower", c, C)):
        for d in range(1, n):
            pl.semaphore_signal(barrier, inc=1, device_id={axis: other(me, d, n)},
                                device_id_type=pl.DeviceIdType.MESH)
    pl.semaphore_wait(barrier, F + T + C - 3)

    w_sems = (lambda d: w_s.at[d]), (lambda d: w_r.at[d])
    gather_start(weight.at[pl.ds(pl.multiple_of(c * kh, 16), kh)], wpart(c), kh, *w_sems)
    partner = 2 * q + 1 - h
    send(texts, tpart(h, c)(f, 0, tr), tp_s.at[0], tp_r.at[0], "tp", partner)
    for e in range(1, C):
        send(texts, tpart(h, c)(f, 0, tr), to_s.at[0, e], to_r.at[0, e], "tower", other(c, e, C))

    img_copy.wait()
    w_copy.wait()
    aligned = kb % 128 == 0

    def by_k(ff):
        k = pl.multiple_of(ff * kb, kb)
        return jnp.dot(img[:, pl.ds(k, kb)], wall[pl.ds(k, kb), :], preferred_element_type=F32)

    if aligned:
        acc[...] = by_k(f)

    def turn(k, carry):
        k = pl.multiple_of(k * 128, 128)
        img_t[pl.ds(k, 128), :] = img[:, pl.ds(k, 128)].T
        return carry

    lax.fori_loop(0, width // 128, turn, 0)

    def wf(d):
        return (lambda e: wf_s.at[d, e]), (lambda e: wf_r.at[d, e])

    def w_from(d):
        gather_wait(d, wpart(c), kh, *w_sems)
        share_out(wpart(c)(fsdp_from(d), 0, kh), *wf(d))

    def w_rest(d):
        ff = fsdp_from(d)
        shared_in(lambda cc: wpart(cc)(ff, 0, kh), *wf(d))
        if aligned:
            acc[...] += by_k(ff)

    def t_sems(k):
        return (lambda d: t_s.at[k, d]), (lambda d: t_r.at[k, d])

    def tf(k, d):
        return (lambda e: tf_s.at[k, d, e]), (lambda e: tf_r.at[k, d, e])

    def to(k):
        return (lambda e: to_s.at[k, e]), (lambda e: to_r.at[k, e])

    sides = (h, 1 - h)
    for d in range(1, F - 1):
        w_from(d)
    gather_start(texts, tpart(h, c), tr, *t_sems(0))
    for d in range(1, F - 1):
        w_rest(d)
    theirs = tpart(1 - h, c)(f, 0, tr)
    arrived(theirs, tp_s.at[0], tp_r.at[0], "tp", partner)
    share_out(theirs, *to(1))
    w_from(F - 1)
    gather_start(theirs, tpart(1 - h, c), tr, *t_sems(1))
    w_rest(F - 1)
    if not aligned:
        acc[...] = jnp.zeros_like(acc)

        def by_tile(k, carry):
            k = pl.multiple_of(k * 128, 128)
            acc[...] += jnp.dot(img[:, pl.ds(k, 128)], wall[pl.ds(k, 128), :],
                                preferred_element_type=F32)
            return carry

        lax.fori_loop(0, width // 128, by_tile, 0)

    for k in range(2):
        eown[k] = acc[k * half : (k + 1) * half, :].astype(BF16)
    for d in range(1, T):
        tt = other(t, d, T)
        send(eown.at[lax.rem(tt, 2)], ebuf.at[t], e_s.at[d], e_r.at[d], "tp", tt)
    ebuf[t] = eown[h]

    def t_from(k, d):
        gather_wait(d, tpart(sides[k], c), tr, *t_sems(k))
        share_out(tpart(sides[k], c)(fsdp_from(d), 0, tr), *tf(k, d))

    def t_rest(k, d):
        ff = fsdp_from(d)
        shared_in(lambda cc: tpart(sides[k], cc)(ff, 0, tr), *tf(k, d))

    t_copy.wait()
    for k in range(2):
        for d in range(1, F - 1):
            t_from(k, d)
    for k in range(2):
        shared_in(lambda cc: tpart(sides[k], cc)(f, 0, tr), *to(k))

    for d in range(1, T):
        tt = other(t, T - d, T)
        arrived(ebuf.at[tt], e_s.at[d], e_r.at[d], "tp", tt)
    square = jnp.zeros((half, 1), F32)
    for k in range(T):
        part = ebuf[k].astype(F32)
        square += jnp.sum(part * part, axis=1, keepdims=True)
    rnorm = lax.rsqrt(square + epsilon)
    for k in range(T):
        ubuf[:, k * cols : (k + 1) * cols] = (ebuf[k].astype(F32) * rnorm).astype(BF16)

    span = pl.ds(pl.multiple_of(h * half, half), half)
    permf, = spread([perm[:, span].astype(F32)], 128)
    lane = lax.broadcasted_iota(jnp.int32, (1, bw), 1)

    def hits(j):
        return permf == ((j * T + 2 * q) * (bw // 2) + lane).astype(F32)

    def score(j, top):
        logit = score_scale * lax.dot_general(ubuf[...], tall[j], NT, preferred_element_type=F32)
        lbuf[j] = logit
        return jnp.maximum(top, jnp.max(logit, axis=1, keepdims=True))

    top = score(f, jnp.full((half, 1), -jnp.inf, F32))
    for d in range(1, F):
        for k in range(2):
            if d == F - 1:
                t_from(k, d)
        for k in range(2):
            t_rest(k, d)
        top = score(fsdp_from(d), top)

    def totals(j, so_far):
        total, first, positive = so_far
        logit = lbuf[j]
        power = jnp.exp(logit - top)
        return (
            total + jnp.sum(power, axis=1, keepdims=True),
            first + jnp.sum(power * logit, axis=1, keepdims=True),
            positive + jnp.sum(jnp.where(hits(j), logit, 0.0), axis=1, keepdims=True),
        )

    zero = jnp.zeros((half, 1), F32)
    total, first, positive = lax.fori_loop(0, F, totals, (zero, zero, zero))
    place = lax.broadcasted_iota(jnp.int32, (half, 128), 1)
    packed = jnp.where(place == 0, top, jnp.where(place == 1, total,
                       jnp.where(place == 2, first, jnp.where(place == 3, positive, rnorm))))
    sbuf[t] = packed.T[:8]
    for d in range(1, T):
        send(sbuf.at[t], sbuf.at[t], st_s.at[d], st_r.at[d], "tp", other(t, d, T))

    def stats_from(d):
        tt = other(t, T - d, T)
        arrived(sbuf.at[tt], st_s.at[d], st_r.at[d], "tp", tt)

    def combined(group):
        peak = sbuf[group, 0:1, :]
        for k in range(1, T // 2):
            peak = jnp.maximum(peak, sbuf[2 * k + group, 0:1, :])
        total = jnp.zeros_like(peak)
        first = jnp.zeros_like(peak)
        positive = jnp.zeros_like(peak)
        for k in range(T // 2):
            scale = jnp.exp(sbuf[2 * k + group, 0:1, :] - peak)
            total += scale * sbuf[2 * k + group, 1:2, :]
            first += scale * sbuf[2 * k + group, 2:3, :]
            positive += sbuf[2 * k + group, 3:4, :]
        return peak + jnp.log(total), first / total, positive

    def sign_of(places):
        return 1.0 - 2.0 * forget[:, places].astype(F32)

    for d in range(2, T, 2):
        stats_from(d)
    lse_row, _, _ = combined(h)
    lse, sign = spread([lse_row, sign_of(span)], 128)

    def weigh(j, carry):
        pbuf[j] = (sign * (jnp.exp(lbuf[j] - lse) - hits(j).astype(F32))).astype(BF16)
        return carry

    lax.fori_loop(0, F, weigh, 0)

    def grad_for(tt):
        place = pl.ds(pl.multiple_of(tt * cols, cols), cols)
        total = jnp.dot(pbuf[0], tall[0, :, place], preferred_element_type=F32)
        for j in range(1, F):
            total += jnp.dot(pbuf[j], tall[j, :, place], preferred_element_type=F32)
        return score_scale * total

    for d in range(1, T):
        tt = other(t, d, T)
        gsend[d] = grad_for(tt).astype(BF16)
        send(gsend.at[d], grecv.at[t], g_s.at[d], g_r.at[d], "tp", tt)
    gown[h] = grad_for(t)
    gown[1 - h] = jnp.zeros((half, cols), F32)
    grecv[t] = jnp.zeros((half, cols), BF16)

    for d in range(1, T, 2):
        stats_from(d)
    kept = []
    for k in range(2):
        places = slice(k * half, (k + 1) * half)
        lse_row, mean_row, positive = combined(k)
        loss[:, places] = lse_row - positive
        kept.append(spread([sign_of(places) * (mean_row - positive), sbuf[k, 4:5, :]], 128))
    for d in range(1, T):
        tt = other(t, T - d, T)
        arrived(grecv.at[tt], g_s.at[d], g_r.at[d], "tp", tt)
    for k in range(2):
        radial, rnorm = kept[k]
        grad = gown[k]
        for j in range(T // 2):
            grad += grecv[2 * j + k].astype(F32)
        unit = eown[k].astype(F32) * rnorm
        gemb[k * half : (k + 1) * half, :] = (rnorm * (grad - unit * radial)).astype(BF16)

    def block(ff, cc):
        k = pl.multiple_of(ff * kb + cc * kh, 16)
        return jnp.dot(img_t[pl.ds(k, kh), :], gemb[...], preferred_element_type=F32)

    def compute(d):
        ff = fsdp_to(d)
        for e in range(1, C):
            cc = other(c, e, C)
            sib_send[d, e] = block(ff, cc)
            send(sib_send.at[d, e], sib_recv.at[d, e], b_s.at[d, e], b_r.at[d, e], "tower", cc)
        share[d] = block(ff, c)

    def joined(d):
        total = share[d]
        for e in range(1, C):
            arrived(sib_recv.at[d, e], b_s.at[d, e], b_r.at[d, e], "tower", other(c, C - e, C))
            total += sib_recv[d, e]
        return total

    def dispatch(d):
        wsend[d] = joined(d).astype(BF16)
        send(wsend.at[d], wrecv.at[d], x_s.at[d], x_r.at[d], "fsdp", fsdp_to(d))

    for d in range(F - 1, 0, -1):
        compute(d)
        if d < F - 1:
            dispatch(d + 1)
    compute(0)
    dispatch(1)
    total = joined(0)
    for d in range(F - 1, 0, -1):
        arrived(wrecv.at[d], x_s.at[d], x_r.at[d], "fsdp", fsdp_from(d))
        total += wrecv[d].astype(F32)
    obuf[c] = total
    share_out(obuf.at[c], lambda e: o_s.at[e], lambda e: o_r.at[e])
    home = pltpu.make_async_copy(obuf.at[c], out.at[c], loc.at[3])
    home.start()
    for e in range(1, C):
        cc = other(c, C - e, C)
        arrived(obuf.at[cc], o_s.at[e], o_r.at[e], "tower", cc)
        away = pltpu.make_async_copy(obuf.at[cc], out.at[cc], loc.at[3 + e])
        away.start()
        away.wait()
    home.wait()
    for copy in sends:
        copy.wait_send()


def local(images, weight, texts, perm, forget):
    F, T, C = lax.axis_size("fsdp"), lax.axis_size("tp"), lax.axis_size("tower")
    assert T % 2 == 0
    pairs, width = images.shape
    kb, cols = weight.shape
    kh = kb // C
    tr, embed = texts.shape
    half = pairs // 2
    bw = 2 * tr * C
    vmem, dma = pltpu.VMEM, pltpu.SemaphoreType.DMA
    scratch = [
        vmem((pairs, width), BF16),
        vmem((width, pairs), BF16),
        vmem((width, cols), BF16),
        vmem((F, bw, embed), BF16),
        vmem((pairs, cols), F32),
        vmem((2, half, cols), BF16),
        vmem((T, half, cols), BF16),
        vmem((half, embed), BF16),
        vmem((F, half, bw), F32),
        vmem((F, half, bw), BF16),
        vmem((T, 8, half), F32),
        vmem((2, half, cols), F32),
        vmem((T, half, cols), BF16),
        vmem((T, half, cols), BF16),
        vmem((pairs, cols), BF16),
        vmem((F, kh, cols), F32),
        vmem((F, C, kh, cols), F32),
        vmem((F, C, kh, cols), F32),
        vmem((F, kh, cols), BF16),
        vmem((F, kh, cols), BF16),
        vmem((C, kh, cols), F32),
        dma((3 + C,)),
        dma((F + 1,)), dma((F + 1,)), dma((F, C)), dma((F, C)),
        dma((2, F + 1)), dma((2, F + 1)), dma((2, F, C)), dma((2, F, C)),
        dma((2, C)), dma((2, C)), dma((1,)), dma((1,)),
        dma((T,)), dma((T,)), dma((T,)), dma((T,)),
        dma((T,)), dma((T,)),
        dma((F, C)), dma((F, C)), dma((F,)), dma((F,)),
        dma((C,)), dma((C,)),
    ]
    any_space = pl.BlockSpec(memory_space=pl.ANY)
    whole = pl.BlockSpec(memory_space=pltpu.VMEM)
    loss, out = pl.pallas_call(
        functools.partial(kernel, (F, T, C)),
        out_shape=(
            jax.ShapeDtypeStruct((1, pairs), F32),
            jax.ShapeDtypeStruct((C, kh, cols), F32),
        ),
        in_specs=[any_space, any_space, any_space, whole, whole],
        out_specs=(whole, any_space),
        scratch_shapes=scratch,
        compiler_params=pltpu.CompilerParams(
            collective_id=0, has_side_effects=True, vmem_limit_bytes=60 * 2**20
        ),
        cost_estimate=pl.CostEstimate(
            flops=4 * pairs * cols * width + 4 * half * F * bw * embed,
            bytes_accessed=2 * (pairs * width + kb * cols + tr * embed) + 4 * kb * cols,
            transcendentals=2 * half * F * bw,
        ),
    )(images, weight, texts, perm.reshape(1, pairs), forget.reshape(1, pairs))
    return loss.reshape(pairs), out.reshape(kb, cols)


def solution(mesh):
    return jax.shard_map(
        local,
        mesh=mesh,
        in_specs=(
            P(("fsdp", "tower"), None),
            P("fsdp", "tp"),
            P(("fsdp", "tp", "tower"), None),
            P(("fsdp", "tower")),
            P(("fsdp", "tower")),
        ),
        out_specs=(P(("fsdp", "tower")), P("fsdp", "tp")),
        check_vma=False,
    )
```

time: 106 us -> 84.7 us (0.80)
  Pallas kernels: 101 us -> 80.2 us
    pallas_call x1, Pallas kernels: 101 us -> 80.2 us  [local(): pl.pallas_call(functools.partial(kernel, (F, T, C)), out_shape=(jax.Shape...]
where the time goes in v2:
time: 84.7 us; the launch traced here: 84.5 us
  Pallas kernels  80.2 us (95%)
  local copies, waits for them, and re-layouts  3.71 us (4%)
    pallas_call x1, Pallas kernels, local(): pl.pallas_call(functools.partial(kernel, (F, T, C)), out_shape=(jax.Shape...  80.2 us
    unnamed x2, local copies, waits for them, and re-layouts  3.71 us

profile of v2, /device:TPU:9, one launch (start us, length us, event | category | flops | bytes accessed | tf_op | source)
XLA Modules:
  0.0 84.5 jit_solution(15291599830419953716)
XLA Ops:
  0.6 80.2 %shard_map.68 = (f32[1,512]{1,0:T(1,128)}, f32[2,640,256]{2,1,0:T(8,128)}) custom-call(bf16[512,5120]{1,0:T(8,128)(2,1)} %images.1, bf16[1280,256]{1,0:T(8,128)(2,1)} %weight.1, bf16[128,1024]{1,0:T(8,128)(2,1)} %texts.1, s32[1,512]{1,0:T(1,128)} %bitcast.6, s32[1,512]{1,0:T(1,128)} %bitcast.7), custom_call_target="tpu_custom_call" | custom-call | flops 4831838208 | bytes 7471104 | tf_op jit(solution)/shard_map/pallas_call | solution.py:417
  80.8 1.3 %copy.9 = f32[512]{0:T(512)} copy(f32[512]{0:T(512)} %bitcast.5) | data formatting | bytes 4096
  82.1 2.5 %copy.10 = f32[1280,256]{1,0:T(8,128)} copy(f32[1280,256]{1,0:T(8,128)} %bitcast.4) | data formatting | bytes 2621440

commit v3 on v2

--- a/solution.py
+++ b/solution.py
@@ -38,6 +38,7 @@
     kh = kb // C
     tr, embed = texts.shape
     bw = 2 * tr * C
+    S, w = gemb.shape[0], gemb.shape[2]
     square_plane = F == 4
     sends = []
 
@@ -298,11 +299,16 @@
 
     for d in range(1, T):
         tt = other(t, d, T)
-        gsend[d] = grad_for(tt).astype(BF16)
-        send(gsend.at[d], grecv.at[t], g_s.at[d], g_r.at[d], "tp", tt)
+        partial = grad_for(tt).astype(BF16)
+        for s in range(S):
+            gsend[d, s] = partial[:, s * w : (s + 1) * w]
+        send(gsend.at[d, 0], grecv.at[t, 0], g_s.at[d, 0], g_r.at[d, 0], "tp", tt)
+    for s in range(1, S):
+        for d in range(1, T):
+            send(gsend.at[d, s], grecv.at[t, s], g_s.at[d, s], g_r.at[d, s], "tp", other(t, d, T))
     gown[h] = grad_for(t)
     gown[1 - h] = jnp.zeros((half, cols), F32)
-    grecv[t] = jnp.zeros((half, cols), BF16)
+    grecv[t] = jnp.zeros((S, half, w), BF16)
 
     for d in range(1, T, 2):
         stats_from(d)
@@ -312,61 +318,104 @@
         lse_row, mean_row, positive = combined(k)
         loss[:, places] = lse_row - positive
         kept.append(spread([sign_of(places) * (mean_row - positive), sbuf[k, 4:5, :]], 128))
-    for d in range(1, T):
-        tt = other(t, T - d, T)
-        arrived(grecv.at[tt], g_s.at[d], g_r.at[d], "tp", tt)
-    for k in range(2):
-        radial, rnorm = kept[k]
-        grad = gown[k]
-        for j in range(T // 2):
-            grad += grecv[2 * j + k].astype(F32)
-        unit = eown[k].astype(F32) * rnorm
-        gemb[k * half : (k + 1) * half, :] = (rnorm * (grad - unit * radial)).astype(BF16)
-
-    def block(ff, cc):
+
+    def block(s, ff, cc):
         k = pl.multiple_of(ff * kb + cc * kh, 16)
-        return jnp.dot(img_t[pl.ds(k, kh), :], gemb[...], preferred_element_type=F32)
-
-    def compute(d):
+        return jnp.dot(img_t[pl.ds(k, kh), :], gemb[s], preferred_element_type=F32)
+
+    def compute(s, d):
         ff = fsdp_to(d)
         for e in range(1, C):
             cc = other(c, e, C)
-            sib_send[d, e] = block(ff, cc)
-            send(sib_send.at[d, e], sib_recv.at[d, e], b_s.at[d, e], b_r.at[d, e], "tower", cc)
-        share[d] = block(ff, c)
-
-    def joined(d):
-        total = share[d]
+            sib_send[s, d, e] = block(s, ff, cc)
+            send(sib_send.at[s, d, e], sib_recv.at[s, d, e], b_s.at[s, d, e], b_r.at[s, d, e],
+                 "tower", cc)
+        share[s, d] = block(s, ff, c)
+
+    def join(s, d):
+        total = share[s, d]
         for e in range(1, C):
-            arrived(sib_recv.at[d, e], b_s.at[d, e], b_r.at[d, e], "tower", other(c, C - e, C))
-            total += sib_recv[d, e]
-        return total
-
-    def dispatch(d):
-        wsend[d] = joined(d).astype(BF16)
-        send(wsend.at[d], wrecv.at[d], x_s.at[d], x_r.at[d], "fsdp", fsdp_to(d))
-
-    for d in range(F - 1, 0, -1):
-        compute(d)
-        if d < F - 1:
-            dispatch(d + 1)
-    compute(0)
-    dispatch(1)
-    total = joined(0)
-    for d in range(F - 1, 0, -1):
-        arrived(wrecv.at[d], x_s.at[d], x_r.at[d], "fsdp", fsdp_from(d))
-        total += wrecv[d].astype(F32)
-    obuf[c] = total
-    share_out(obuf.at[c], lambda e: o_s.at[e], lambda e: o_r.at[e])
-    home = pltpu.make_async_copy(obuf.at[c], out.at[c], loc.at[3])
-    home.start()
-    for e in range(1, C):
-        cc = other(c, C - e, C)
-        arrived(obuf.at[cc], o_s.at[e], o_r.at[e], "tower", cc)
-        away = pltpu.make_async_copy(obuf.at[cc], out.at[cc], loc.at[3 + e])
-        away.start()
-        away.wait()
-    home.wait()
+            arrived(sib_recv.at[s, d, e], b_s.at[s, d, e], b_r.at[s, d, e],
+                    "tower", other(c, C - e, C))
+            total += sib_recv[s, d, e]
+        share[s, d] = total
+
+    hh = kh // 2
+
+    def put(s, slot, value, target):
+        wsend[s, slot] = value.astype(BF16)
+        send(wsend.at[s, slot], wrecv.at[s, slot], x_s.at[s, slot], x_r.at[s, slot], "fsdp", target)
+
+    def got(s, slot, source):
+        arrived(wrecv.at[s, slot], x_s.at[s, slot], x_r.at[s, slot], "fsdp", source)
+        return wrecv[s, slot].astype(F32)
+
+    def scatter(s):
+        for d in range(1, T):
+            tt = other(t, T - d, T)
+            arrived(grecv.at[tt, s], g_s.at[d, s], g_r.at[d, s], "tp", tt)
+        places = slice(s * w, (s + 1) * w)
+        for k in range(2):
+            radial, rnorm = kept[k]
+            grad = gown[k, :, places]
+            for j in range(T // 2):
+                grad += grecv[2 * j + k, s].astype(F32)
+            unit = eown[k, :, places].astype(F32) * rnorm
+            gemb[s, k * half : (k + 1) * half, :] = (rnorm * (grad - unit * radial)).astype(BF16)
+        if not square_plane:
+            for d in range(F - 1, 0, -1):
+                compute(s, d)
+                if d < F - 1:
+                    join(s, d + 1)
+                    for k in range(2):
+                        put(s, 2 * (d + 1) + k, share[s, d + 1, k * hh : (k + 1) * hh], fsdp_to(d + 1))
+            compute(s, 0)
+            join(s, 1)
+            for k in range(2):
+                put(s, 2 + k, share[s, 1, k * hh : (k + 1) * hh], fsdp_to(1))
+            return
+        compute(s, 3)
+        compute(s, 1)
+        join(s, 3)
+        put(s, 6, share[s, 3, :hh], fsdp_to(1))
+        put(s, 7, share[s, 3, hh:], fsdp_to(2))
+        compute(s, 2)
+        join(s, 1)
+        put(s, 2, share[s, 1, :hh], fsdp_to(1))
+        compute(s, 0)
+        join(s, 2)
+        put(s, 5, share[s, 2, hh:], fsdp_to(2))
+        put(s, 3, share[s, 1, hh:] + got(s, 7, fsdp_from(2)), fsdp_to(1))
+        put(s, 4, share[s, 2, :hh] + got(s, 6, fsdp_from(1)), fsdp_to(2))
+
+    def o_sems(s):
+        return (lambda e: o_s.at[s, e]), (lambda e: o_r.at[s, e])
+
+    def home(s, cc, k):
+        copy = pltpu.make_async_copy(
+            obuf.at[s, cc], out.at[cc, :, pl.ds(s * w, w)], loc.at[3 + s * C + k])
+        copy.start()
+        return copy
+
+    for s in range(S):
+        scatter(s)
+    homes = []
+    for s in range(S):
+        join(s, 0)
+        for k in range(2):
+            total = share[s, 0, k * hh : (k + 1) * hh]
+            for d in range(1, 3 if square_plane else F):
+                total += got(s, 2 * d + k, fsdp_from(d))
+            obuf[s, c, k * hh : (k + 1) * hh, :] = total
+        share_out(obuf.at[s, c], *o_sems(s))
+        homes.append(home(s, c, 0))
+    for s in range(S):
+        for e in range(1, C):
+            cc = other(c, C - e, C)
+            arrived(obuf.at[s, cc], o_s.at[s, e], o_r.at[s, e], "tower", cc)
+            homes.append(home(s, cc, e))
+    for copy in homes:
+        copy.wait()
     for copy in sends:
         copy.wait_send()
 
@@ -380,6 +429,8 @@
     tr, embed = texts.shape
     half = pairs // 2
     bw = 2 * tr * C
+    S = 2 if cols % 256 == 0 else 1
+    w = cols // S
     vmem, dma = pltpu.VMEM, pltpu.SemaphoreType.DMA
     scratch = [
         vmem((pairs, width), BF16),
@@ -394,23 +445,23 @@
         vmem((F, half, bw), BF16),
         vmem((T, 8, half), F32),
         vmem((2, half, cols), F32),
-        vmem((T, half, cols), BF16),
-        vmem((T, half, cols), BF16),
-        vmem((pairs, cols), BF16),
-        vmem((F, kh, cols), F32),
-        vmem((F, C, kh, cols), F32),
-        vmem((F, C, kh, cols), F32),
-        vmem((F, kh, cols), BF16),
-        vmem((F, kh, cols), BF16),
-        vmem((C, kh, cols), F32),
-        dma((3 + C,)),
+        vmem((T, S, half, w), BF16),
+        vmem((T, S, half, w), BF16),
+        vmem((S, pairs, w), BF16),
+        vmem((S, F, kh, w), F32),
+        vmem((S, F, C, kh, w), F32),
+        vmem((S, F, C, kh, w), F32),
+        vmem((S, 2 * F, kh // 2, w), BF16),
+        vmem((S, 2 * F, kh // 2, w), BF16),
+        vmem((S, C, kh, w), F32),
+        dma((3 + S * C,)),
         dma((F + 1,)), dma((F + 1,)), dma((F, C)), dma((F, C)),
         dma((2, F + 1)), dma((2, F + 1)), dma((2, F, C)), dma((2, F, C)),
         dma((2, C)), dma((2, C)), dma((1,)), dma((1,)),
         dma((T,)), dma((T,)), dma((T,)), dma((T,)),
-        dma((T,)), dma((T,)),
-        dma((F, C)), dma((F, C)), dma((F,)), dma((F,)),
-        dma((C,)), dma((C,)),
+        dma((T, S)), dma((T, S)),
+        dma((S, F, C)), dma((S, F, C)), dma((S, 2 * F)), dma((S, 2 * F)),
+        dma((S, C)), dma((S, C)),
     ]
     any_space = pl.BlockSpec(memory_space=pl.ANY)
     whole = pl.BlockSpec(memory_space=pltpu.VMEM)

time: 84.7 us -> 79.7 us (0.941)
  Pallas kernels: 80.2 us -> 75.1 us
    pallas_call x1, Pallas kernels: 80.2 us -> 75.1 us  [local(): pl.pallas_call(functools.partial(kernel, (F, T, C)), out_shape=(jax.Shape...]
where the time goes in v3:
time: 79.7 us; the launch traced here: 79.5 us
  Pallas kernels  75.1 us (94%)
  local copies, waits for them, and re-layouts  3.71 us (5%)
    pallas_call x1, Pallas kernels, local(): pl.pallas_call(functools.partial(kernel, (F, T, C)), out_shape=(jax.Shape...  75.1 us
    unnamed x2, local copies, waits for them, and re-layouts  3.71 us

profile of v3, /device:TPU:9, one launch (start us, length us, event | category | flops | bytes accessed | tf_op | source)
XLA Modules:
  0.0 79.5 jit_solution(6053700058191998142)
XLA Ops:
  0.6 75.1 %shard_map.68 = (f32[1,512]{1,0:T(1,128)}, f32[2,640,256]{2,1,0:T(8,128)}) custom-call(bf16[512,5120]{1,0:T(8,128)(2,1)} %images.1, bf16[1280,256]{1,0:T(8,128)(2,1)} %weight.1, bf16[128,1024]{1,0:T(8,128)(2,1)} %texts.1, s32[1,512]{1,0:T(1,128)} %bitcast.6, s32[1,512]{1,0:T(1,128)} %bitcast.7), custom_call_target="tpu_custom_call" | custom-call | flops 4831838208 | bytes 7471104 | tf_op jit(solution)/shard_map/pallas_call | solution.py:468
  75.8 1.3 %copy.9 = f32[512]{0:T(512)} copy(f32[512]{0:T(512)} %bitcast.5) | data formatting | bytes 4096
  77.0 2.5 %copy.10 = f32[1280,256]{1,0:T(8,128)} copy(f32[1280,256]{1,0:T(8,128)} %bitcast.4) | data formatting | bytes 2621440

commit v4 on v3

--- a/solution.py
+++ b/solution.py
@@ -138,7 +138,8 @@
         img_t[pl.ds(k, 128), :] = img[:, pl.ds(k, 128)].T
         return carry
 
-    lax.fori_loop(0, width // 128, turn, 0)
+    early = width // 256
+    lax.fori_loop(0, early, turn, 0)
 
     def wf(d):
         return (lambda e: wf_s.at[d, e]), (lambda e: wf_r.at[d, e])
@@ -225,38 +226,39 @@
     def hits(j):
         return permf == ((j * T + 2 * q) * (bw // 2) + lane).astype(F32)
 
-    def score(j, top):
-        logit = score_scale * lax.dot_general(ubuf[...], tall[j], NT, preferred_element_type=F32)
-        lbuf[j] = logit
-        return jnp.maximum(top, jnp.max(logit, axis=1, keepdims=True))
-
-    top = score(f, jnp.full((half, 1), -jnp.inf, F32))
+    def score(j, so_far):
+        top, total, first, positive = so_far
+        lbuf[j] = score_scale * lax.dot_general(
+            ubuf[...], tall[j], NT, preferred_element_type=F32)
+        logit = lbuf[j]
+        peak = jnp.maximum(top, jnp.max(logit, axis=1, keepdims=True))
+        scale = jnp.exp(top - peak)
+        power = jnp.exp(logit - peak)
+        return (
+            peak,
+            total * scale + jnp.sum(power, axis=1, keepdims=True),
+            first * scale + jnp.sum(power * logit, axis=1, keepdims=True),
+            positive + jnp.sum(jnp.where(hits(j), logit, 0.0), axis=1, keepdims=True),
+        )
+
+    zero = jnp.zeros((half, 1), F32)
+    so_far = score(f, (jnp.full((half, 1), -jnp.inf, F32), zero, zero, zero))
     for d in range(1, F):
-        for k in range(2):
-            if d == F - 1:
+        if d == F - 1:
+            for k in range(2):
                 t_from(k, d)
         for k in range(2):
             t_rest(k, d)
-        top = score(fsdp_from(d), top)
-
-    def totals(j, so_far):
-        total, first, positive = so_far
-        logit = lbuf[j]
-        power = jnp.exp(logit - top)
-        return (
-            total + jnp.sum(power, axis=1, keepdims=True),
-            first + jnp.sum(power * logit, axis=1, keepdims=True),
-            positive + jnp.sum(jnp.where(hits(j), logit, 0.0), axis=1, keepdims=True),
-        )
-
-    zero = jnp.zeros((half, 1), F32)
-    total, first, positive = lax.fori_loop(0, F, totals, (zero, zero, zero))
+        so_far = score(fsdp_from(d), so_far)
+    top, total, first, positive = so_far
     place = lax.broadcasted_iota(jnp.int32, (half, 128), 1)
     packed = jnp.where(place == 0, top, jnp.where(place == 1, total,
                        jnp.where(place == 2, first, jnp.where(place == 3, positive, rnorm))))
     sbuf[t] = packed.T[:8]
-    for d in range(1, T):
+    for d in (*range(2, T, 2), *range(1, T, 2)):
         send(sbuf.at[t], sbuf.at[t], st_s.at[d], st_r.at[d], "tp", other(t, d, T))
+
+    lax.fori_loop(early, width // 128, turn, 0)
 
     def stats_from(d):
         tt = other(t, T - d, T)

time: 79.7 us -> 78.6 us (0.986)
  Pallas kernels: 75.1 us -> 74 us
    pallas_call x1, Pallas kernels: 75.1 us -> 74 us  [local(): pl.pallas_call(functools.partial(kernel, (F, T, C)), out_shape=(jax.Shape...]
where the time goes in v4:
time: 78.6 us; the launch traced here: 78.4 us
  Pallas kernels  74 us (94%)
  local copies, waits for them, and re-layouts  3.71 us (5%)
    pallas_call x1, Pallas kernels, local(): pl.pallas_call(functools.partial(kernel, (F, T, C)), out_shape=(jax.Shape...  74 us
    unnamed x2, local copies, waits for them, and re-layouts  3.71 us

profile of v4, /device:TPU:9, one launch (start us, length us, event | category | flops | bytes accessed | tf_op | source)
XLA Modules:
  0.0 78.4 jit_solution(9142372560829628663)
XLA Ops:
  0.6 74.0 %shard_map.68 = (f32[1,512]{1,0:T(1,128)}, f32[2,640,256]{2,1,0:T(8,128)}) custom-call(bf16[512,5120]{1,0:T(8,128)(2,1)} %images.1, bf16[1280,256]{1,0:T(8,128)(2,1)} %weight.1, bf16[128,1024]{1,0:T(8,128)(2,1)} %texts.1, s32[1,512]{1,0:T(1,128)} %bitcast.6, s32[1,512]{1,0:T(1,128)} %bitcast.7), custom_call_target="tpu_custom_call" | custom-call | flops 4831838208 | bytes 7471104 | tf_op jit(solution)/shard_map/pallas_call | solution.py:470
  74.7 1.3 %copy.9 = f32[512]{0:T(512)} copy(f32[512]{0:T(512)} %bitcast.5) | data formatting | bytes 4096
  75.9 2.5 %copy.10 = f32[1280,256]{1,0:T(8,128)} copy(f32[1280,256]{1,0:T(8,128)} %bitcast.4) | data formatting | bytes 2621440
